TPU v7x, 32 devices: a whole 2x2x4 slice. The times are simulated.
32 devices in a mesh: dp: 4 (over y, x), mp: 8 (over z, core).
Axes of the slice: x: 2, y: 2, z: 4, core: 2. Of those that a mesh axis runs over, the one named last changes fastest.
Arguments:
- activations: bfloat16 [4096, 2048], P('dp', 'mp'), may hold values from -6 to 6
- out_grad: bfloat16 [4096, 8192], P('dp'), may hold values from -0.8984375 to 0.8984375
- old_weight: bfloat16 [8, 256, 8192], P('mp', 'dp'), may hold values from -0.125 to 0.125
- old_first: float32 [8, 256, 8192], P('mp', 'dp'), may hold values from -6 to 6
- old_second: float32 [8, 256, 8192], P('mp', 'dp'), may hold values from 0.25 to 4
- step: int32 [1], replicated, may hold values from 1 to 31
- next_input: bfloat16 [4096, 2048], P('dp', 'mp'), may hold values from -6 to 6
Outputs:
- new_weight: bfloat16 [8, 344, 8192], P('mp', 'dp')
- new_first: float32 [8, 344, 8192], P('mp', 'dp')
- new_second: float32 [8, 344, 8192], P('mp', 'dp')
- output: bfloat16 [4096, 8192], P('dp', 'mp')
Inputs may be any that keep to these rules, and one draw needn't show every extreme that they name: `step`: the number of Adam steps taken, this one included.
All inputs are finite; a program needn't handle non-finite values.
Results may differ from a plain program's by a relative error of at most 0.0049.
Values may be sent and summed in bfloat16 or wider, within the bound.
A program may use at most 192 MiB of HBM per device.

v0:
```python
import jax
import jax.numpy as jnp
from jax import lax
from jax.sharding import PartitionSpec as P


def partner(i, k, n):
    return i ^ k if n & n - 1 == 0 else (i + k) % n


def exchange(block, axis, k):
    n = lax.axis_size(axis)
    return lax.ppermute(block, axis, [(i, partner(i, k, n)) for i in range(n)])


def target(k, n, axis):
    me = lax.axis_index(axis)
    return me ^ k if n & n - 1 == 0 else lax.rem(me + k, n)


def to_front(block, axis):
    n = lax.axis_size(axis)
    return lax.ppermute(block, axis, [(i, i - 1) for i in range(1, n)])


def body(activations, out_grad, old_weight, old_first, old_second, step, next_input):
    owners = lax.axis_size("dp")
    owner = lax.axis_index("dp")
    old_rows = old_weight.shape[1]
    width = old_weight.shape[2]
    held_rows = old_rows * owners
    shard_rows = (held_rows + owners - 2) // (owners - 1)
    input_all = lax.all_gather(next_input, "mp", axis=1, tiled=True)
    part = lax.dot_general(
        activations, out_grad, (((0,), (0,)), ((), ())), preferred_element_type=jnp.float32
    ).astype(jnp.bfloat16)
    part = part.reshape(owners, old_rows, width)
    grad = lax.dynamic_index_in_dim(part, owner, 0, keepdims=False).astype(jnp.float32)
    for k in range(1, owners):
        away = lax.dynamic_index_in_dim(part, target(k, owners, "dp"), 0, keepdims=False)
        grad = grad + exchange(away, "dp", k).astype(jnp.float32)
    step_float = step[0].astype(jnp.float32)
    first_fix = 1.0 - jnp.power(jnp.float32(0.9), step_float)
    second_fix = 1.0 - jnp.power(jnp.float32(0.95), step_float)
    new_first = 0.9 * old_first[0] + 0.1 * grad
    new_second = 0.95 * old_second[0] + 0.05 * grad * grad
    update = new_first / first_fix / (jnp.sqrt(new_second / second_fix) + 1e-08)
    new_weight = (old_weight[0].astype(jnp.float32) - 0.01 * update).astype(jnp.bfloat16)
    weight_part = lax.all_to_all(new_weight, "mp", split_axis=1, concat_axis=0, tiled=True)
    heads = lax.axis_size("mp")
    weight_part = weight_part.reshape(heads, old_rows, -1)
    weight_cols = lax.all_gather(weight_part, "dp", axis=1, tiled=True)
    weight_cols = weight_cols.reshape(heads * held_rows, -1)
    begin = owner * (shard_rows - old_rows)

    def mine(block):
        behind = to_front(block.astype(jnp.bfloat16), "dp").astype(block.dtype)
        rows = jnp.concatenate([block, behind, jnp.zeros((shard_rows, width), block.dtype)], 0)
        return lax.dynamic_slice_in_dim(rows, begin, shard_rows, 0)[None]

    outs = (mine(new_weight), mine(new_first), mine(new_second))
    output = jnp.dot(input_all, weight_cols, preferred_element_type=jnp.float32).astype(
        jnp.bfloat16
    )
    return (*outs, output)


def solution(mesh):
    return jax.shard_map(
        body,
        mesh=mesh,
        in_specs=(
            P("dp", "mp"),
            P("dp", None),
            P("mp", "dp", None),
            P("mp", "dp", None),
            P("mp", "dp", None),
            P(),
            P("dp", "mp"),
        ),
        out_specs=(P("mp", "dp", None), P("mp", "dp", None), P("mp", "dp", None), P("dp", "mp")),
        check_vma=False,
    )
```

profile of v0, /device:TPU:0, one launch (start us, length us, event | category | flops | bytes accessed | tf_op | source)
XLA Modules:
  0.0 292.9 jit_solution(17170010049314651664)
XLA Ops:
  7.2 0.0 copy-start
  7.2 0.0 all-gather.3.cloned.1.call-start
  7.2 1.0 copy-done
  8.2 10.7 %convolution_convert_fusion = bf16[256,8192]{1,0:T(8,128)(2,1)S(1)} fusion(bf16[1024,256]{1,0:T(8,128)(2,1)S(1)} %copy-done, bf16[1024,8192]{1,0:T(8,128)(2,1)} %param.8), kind=kOutput, calls=%fused_computation | convolution fusion | flops 4297064448 | bytes 21495808 | tf_op jit(solution)/shard_map/dot_general | solution.py:34
  19.0 0.0 copy-start.4
  19.0 1.8 dynamic-slice_bitcast_fusion.2
  20.7 1.2 copy-done.4
  21.9 2.9 %collective-permute-start = (bf16[64,8192]{1,0:T(8,128)(2,1)}, bf16[64,8192]{1,0:T(8,128)(2,1)S(1)}, u32[]{:S(2)}, u32[]{:S(2)}) collective-permute-start(bf16[64,8192]{1,0:T(8,128)(2,1)} %get-tuple-element.26), channel_id=1, source_target_pairs={{0,8},{8,0},{16,24},{24,16},{1,9},{9,1},{17,25},{25,17},{2,10},{10... | collective-permute-start | bytes 3145736 | tf_op jit(solution)/shard_map/ppermute | solution.py:13
  24.8 1.5 collective-permute-start.1
  26.4 0.0 collective-permute-start.2
  27.1 0.0 copy-start.9
  27.1 21.9 %collective-permute-done = bf16[64,8192]{1,0:T(8,128)(2,1)S(1)} collective-permute-done((bf16[64,8192]{1,0:T(8,128)(2,1)}, bf16[64,8192]{1,0:T(8,128)(2,1)S(1)}, u32[]{:S(2)}, u32[]{:S(2)}) %collective-permute-start) | collective-permute-done | bytes 1048608 | tf_op jit(solution)/shard_map/ppermute | solution.py:13
  49.0 23.1 %collective-permute-done.1 = bf16[64,8192]{1,0:T(8,128)(2,1)S(1)} collective-permute-done((bf16[64,8192]{1,0:T(8,128)(2,1)}, bf16[64,8192]{1,0:T(8,128)(2,1)S(1)}, u32[]{:S(2)}, u32[]{:S(2)}) %collective-permute-start.1) | collective-permute-done | bytes 1048608 | tf_op jit(solution)/shard_map/ppermute | solution.py:13
  72.1 0.0 copy-done.7
  72.2 1.0 copy-done.8
  73.1 0.0 collective-permute-done.2
  73.1 5.9 %fusion.11 = (bf16[64,8192]{1,0:T(8,128)(2,1)}, f32[64,8192]{1,0:T(8,128)S(1)}, bf16[64,8192]{1,0:T(8,128)(2,1)}, f32[64,8192]{1,0:T(8,128)S(1)}) fusion(bf16[64,8192]{1,0:T(8,128)(2,1)} %collective-permute-done.2, bf16[64,8192]{1,0:T(8,128)(2,1)} %copy-done.8, bf16[64,8192]{1,0:T(8,128)(2,1)} %copy-done.7, bf16[4,64,8192]{2,1,0:T(8,128)(2,1)} %bitcast.42, ...), kind=kLoop, calls=%fused_computation.29 | loop fusion | flops 8388608 | bytes 14680068 | tf_op jit(solution)/shard_map/convert_element_type | solution.py:57
  79.0 0.0 copy-done.9
  79.0 1.1 fusion.7
  80.1 0.2 copy-done.2
  80.3 0.1 copy.21
  80.4 31.3 %all_to_all.16 = bf16[64,8,1024]{2,0,1:T(8,128)(2,1)S(1)} all-to-all(bf16[64,8,1024]{2,0,1:T(8,128)(2,1)S(1)} %bitcast.46), channel_id=1, replica_groups=mesh['dp'=4,'mp'=8] {'mp'}, dimensions={1} | all-to-all | bytes 2097152 | tf_op jit(solution)/shard_map/all_to_all | solution.py:49
  111.7 1.5 copy.16
  113.2 0.0 all-gather.3.cloned.1.call-update
  113.2 0.0 all-gather.5.cloned.1.call-start
  113.3 0.7 all-gather.5.cloned.1.call-update
  114.0 1.3 collective-permute-start.4
  115.3 1.3 collective-permute-start.5
  116.6 0.1 pad_dynamic-slice_fusion.6
  116.7 0.1 pad_dynamic-slice_fusion.7
  116.8 1.5 collective-permute-start.3
  118.2 35.3 %collective-permute-done.4 = bf16[64,8192]{1,0:T(8,128)(2,1)} collective-permute-done((bf16[64,8192]{1,0:T(8,128)(2,1)}, bf16[64,8192]{1,0:T(8,128)(2,1)}, u32[]{:S(2)}, u32[]{:S(2)}) %collective-permute-start.4) | collective-permute-done | bytes 1048608 | tf_op jit(solution)/shard_map/ppermute | solution.py:23
  153.5 1.4 convert_element_type.60
  154.9 0.0 copy-start.3
  154.9 21.1 %collective-permute-done.5 = bf16[64,8192]{1,0:T(8,128)(2,1)} collective-permute-done((bf16[64,8192]{1,0:T(8,128)(2,1)}, bf16[64,8192]{1,0:T(8,128)(2,1)}, u32[]{:S(2)}, u32[]{:S(2)}) %collective-permute-start.5) | collective-permute-done | bytes 1048608 | tf_op jit(solution)/shard_map/ppermute | solution.py:23
  176.0 1.4 convert_element_type.62
  177.4 0.0 copy-done.3
  177.4 4.0 %fusion.1 = (f32[86,8192]{1,0:T(8,128)}, f32[86,8192]{1,0:T(8,128)}) fusion(s32[]{:T(128)S(6)} %select_n.22, f32[64,8192]{1,0:T(8,128)S(1)} %get-tuple-element.21, f32[64,8192]{1,0:T(8,128)S(1)} %convert_element_type.62, f32[86]{0:T(128)S(1)} %pad_dynamic-slice_fusion.6, f32[64,8192]{1,0:T(8,128)S(1)} %convert_element_type.60, f32[64,8192]{1,0:T(8,128)S(1)} %copy-done.3), kind=kLoop, calls=%fused_computation.9 | loop fusion | flops 2818048 | bytes 14025052 | tf_op jit(solution)/shard_map/concatenate | solution.py:58
  181.3 6.7 %broadcast_in_dim.14 = f32[1,86,8192]{2,0,1:T(1,128)} reshape(f32[86,8192]{1,0:T(8,128)} %get-tuple-element.30) | data formatting | bytes 5636096 | tf_op jit(solution)/shard_map/broadcast_in_dim | solution.py:59
  188.0 0.0 copy-done.5
  188.0 4.7 %broadcast_in_dim.15 = f32[1,86,8192]{2,0,1:T(1,128)} reshape(f32[86,8192]{1,0:T(8,128)S(1)} %copy-done.5) | data formatting | bytes 5636096 | tf_op jit(solution)/shard_map/broadcast_in_dim | solution.py:59
  192.8 4.1 %collective-permute-done.3 = bf16[64,8192]{1,0:T(8,128)(2,1)} collective-permute-done((bf16[64,8192]{1,0:T(8,128)(2,1)}, bf16[64,8192]{1,0:T(8,128)(2,1)}, u32[]{:S(2)}, u32[]{:S(2)}) %collective-permute-start.3) | collective-permute-done | bytes 1048608 | tf_op jit(solution)/shard_map/ppermute | solution.py:23
  196.9 3.4 %fusion.10 = bf16[1,86,8192]{2,1,0:T(8,128)(2,1)} fusion(s32[]{:T(128)S(6)} %select_n.22, bf16[64,8192]{1,0:T(8,128)(2,1)} %copy-done.6, bf16[64,8192]{1,0:T(8,128)(2,1)} %collective-permute-done.3, bf16[86]{0:T(256)(128)(2,1)S(1)} %pad_dynamic-slice_fusion.7), kind=kLoop, calls=%fused_computation.22 | loop fusion | flops 4227072 | bytes 3506352 | tf_op jit(solution)/shard_map/broadcast_in_dim | solution.py:59
  200.3 25.5 %all-gather.3.cloned.1.call-done = bf16[8,256,1024]{2,0,1:T(8,128)(2,1)} async-done(((bf16[8,64,1024]{2,0,1:T(8,128)(2,1)}), bf16[8,256,1024]{2,0,1:T(8,128)(2,1)}) %all-gather.3.cloned.1.call-update) | async-done | bytes 4194320 | tf_op jit(solution)/shard_map/all_gather | solution.py:52
  225.8 6.5 %copy.17 = bf16[8,256,1024]{2,1,0:T(8,128)(2,1)} copy(bf16[8,256,1024]{2,0,1:T(8,128)(2,1)} %all-gather.3.cloned.1.call-done) | data formatting | bytes 8388608 | tf_op jit(solution)/shard_map/all_gather | solution.py:52
  232.3 42.9 %all-gather.5.cloned.1.call-done = bf16[1024,2048]{1,0:T(8,128)(2,1)} async-done(((bf16[1024,256]{1,0:T(8,128)(2,1)}), bf16[1024,2048]{1,0:T(8,128)(2,1)}) %all-gather.5.cloned.1.call-update) | async-done | bytes 4194320 | tf_op jit(solution)/shard_map/all_gather | solution.py:33
  275.2 8.3 %convert_bitcast_fusion = bf16[1024,1024]{0,1:T(8,128)(2,1)S(1)} fusion(bf16[2048,1024]{1,0:T(8,128)(2,1)} %bitcast.44, bf16[1024,2048]{1,0:T(8,128)(2,1)} %all-gather.5.cloned.1.call-done), kind=kOutput, calls=%fused_computation.19 | convolution fusion | flops 4296015872 | bytes 10485760 | tf_op jit(solution)/shard_map/dot_general | solution.py:62
  283.5 2.6 copy.18
  (10 shorter events, 0.0 us)
Async XLA Ops:
  7.2 1.1 copy-start
  7.2 218.6 %all-gather.3.cloned.1.call-start = ((), (), s32[]{:S(2)}) async-start(), calls=%async_computation.1 | async-start | bytes 5242880 | tf_op jit(solution)/shard_map/all_gather | solution.py:52
  19.0 2.9 %copy-start.4 = (bf16[256,8192]{1,0:T(8,128)(2,1)}, bf16[256,8192]{1,0:T(8,128)(2,1)S(1)}, u32[]{:S(2)}) copy-start(bf16[256,8192]{1,0:T(8,128)(2,1)S(1)} %convolution_convert_fusion) | copy-start | bytes 12582916
  21.9 27.1 %collective-permute-start = (bf16[64,8192]{1,0:T(8,128)(2,1)}, bf16[64,8192]{1,0:T(8,128)(2,1)S(1)}, u32[]{:S(2)}, u32[]{:S(2)}) collective-permute-start(bf16[64,8192]{1,0:T(8,128)(2,1)} %get-tuple-element.26), channel_id=1, source_target_pairs={{0,8},{8,0},{16,24},{24,16},{1,9},{9,1},{17,25},{25,17},{2,10},{10... | collective-permute-start | bytes 3145736 | tf_op jit(solution)/shard_map/ppermute | solution.py:13
  24.8 47.3 %collective-permute-start.1 = (bf16[64,8192]{1,0:T(8,128)(2,1)}, bf16[64,8192]{1,0:T(8,128)(2,1)S(1)}, u32[]{:S(2)}, u32[]{:S(2)}) collective-permute-start(bf16[64,8192]{1,0:T(8,128)(2,1)} %get-tuple-element.28), channel_id=1, source_target_pairs={{0,16},{8,24},{16,0},{24,8},{1,17},{9,25},{17,1},{25,9},{2,18},{10... | collective-permute-start | bytes 3145736 | tf_op jit(solution)/shard_map/ppermute | solution.py:13
  26.4 46.8 %collective-permute-start.2 = (bf16[64,8192]{1,0:T(8,128)(2,1)}, bf16[64,8192]{1,0:T(8,128)(2,1)}, u32[]{:S(2)}, u32[]{:S(2)}) collective-permute-start(bf16[64,8192]{1,0:T(8,128)(2,1)} %get-tuple-element.27), channel_id=1, source_target_pairs={{0,24},{8,16},{16,8},{24,0},{1,25},{9,17},{17,9},{25,1},{2,26},{10... | collective-permute-start | bytes 3145736 | tf_op jit(solution)/shard_map/ppermute | solution.py:13
  27.1 51.9 %copy-start.9 = (bf16[1,64,8192]{2,1,0:T(8,128)(2,1)S(1)}, bf16[1,64,8192]{2,1,0:T(8,128)(2,1)}, u32[]{:S(2)}) copy-start(bf16[1,64,8192]{2,1,0:T(8,128)(2,1)} %param.9) | copy-start | bytes 3145732
  49.0 23.1 %copy-start.7 = (bf16[64,8192]{1,0:T(8,128)(2,1)}, bf16[64,8192]{1,0:T(8,128)(2,1)S(1)}, u32[]{:S(2)}) copy-start(bf16[64,8192]{1,0:T(8,128)(2,1)S(1)} %collective-permute-done) | copy-start | bytes 3145732
  72.2 1.0 copy-start.8
  79.0 1.3 copy-start.2
  80.3 31.4 %copy-start.6 = (bf16[64,8192]{1,0:T(8,128)(2,1)}, bf16[64,8192]{1,0:T(8,128)(2,1)S(1)}, u32[]{:S(2)}) copy-start(bf16[64,8192]{1,0:T(8,128)(2,1)S(1)} %fusion.7) | copy-start | bytes 3145732
  113.2 162.0 %all-gather.5.cloned.1.call-start = ((), (), s32[]{:S(2)}) async-start(), calls=%async_computation.2 | async-start | bytes 4718592 | tf_op jit(solution)/shard_map/all_gather | solution.py:33
  114.0 39.5 %collective-permute-start.4 = (bf16[64,8192]{1,0:T(8,128)(2,1)}, bf16[64,8192]{1,0:T(8,128)(2,1)}, u32[]{:S(2)}, u32[]{:S(2)}) collective-permute-start(bf16[64,8192]{1,0:T(8,128)(2,1)} %get-tuple-element.24), channel_id=1, source_target_pairs={{8,0},{16,8},{24,16},{9,1},{17,9},{25,17},{10,2},{18,10},{26,18},{... | collective-permute-start | bytes 3145736 | tf_op jit(solution)/shard_map/ppermute | solution.py:23
  115.3 60.7 %collective-permute-start.5 = (bf16[64,8192]{1,0:T(8,128)(2,1)}, bf16[64,8192]{1,0:T(8,128)(2,1)}, u32[]{:S(2)}, u32[]{:S(2)}) collective-permute-start(bf16[64,8192]{1,0:T(8,128)(2,1)} %get-tuple-element.20), channel_id=1, source_target_pairs={{8,0},{16,8},{24,16},{9,1},{17,9},{25,17},{10,2},{18,10},{26,18},{... | collective-permute-start | bytes 3145736 | tf_op jit(solution)/shard_map/ppermute | solution.py:23
  116.8 80.1 %collective-permute-start.3 = (bf16[64,8192]{1,0:T(8,128)(2,1)}, bf16[64,8192]{1,0:T(8,128)(2,1)}, u32[]{:S(2)}, u32[]{:S(2)}) collective-permute-start(bf16[64,8192]{1,0:T(8,128)(2,1)} %copy-done.6), channel_id=1, source_target_pairs={{8,0},{16,8},{24,16},{9,1},{17,9},{25,17},{10,2},{18,10},{26,18},{... | collective-permute-start | bytes 3145736 | tf_op jit(solution)/shard_map/ppermute | solution.py:23
  154.9 22.5 %copy-start.3 = (f32[64,8192]{1,0:T(8,128)S(1)}, f32[64,8192]{1,0:T(8,128)}, u32[]{:S(2)}) copy-start(f32[64,8192]{1,0:T(8,128)} %copy-done.2) | copy-start | bytes 6291460
  181.3 6.7 %copy-start.5 = (f32[86,8192]{1,0:T(8,128)S(1)}, f32[86,8192]{1,0:T(8,128)}, u32[]{:S(2)}) copy-start(f32[86,8192]{1,0:T(8,128)} %get-tuple-element.29) | copy-start | bytes 8454148
  275.2 10.9 %copy-start.1 = (bf16[1024,256]{1,0:T(8,128)(2,1)S(1)}, bf16[1024,256]{1,0:T(8,128)(2,1)}, u32[]{:S(2)}) copy-start(bf16[1024,256]{1,0:T(8,128)(2,1)} %param.7) | copy-start | bytes 1572868
Sparse Core Ops, SparseCore 0:
  113.3 112.3 all-gather.2
  227.4 47.7 all-gather.4
where the time goes:
time: 293 us
  waiting for transfers between devices  175 us (60%)
  blocking collectives  31.3 us (11%)
  local copies, waits for them, and re-layouts  27.4 us (9%)
  matrix products  19 us (6%)
  other arithmetic  17 us (6%)
  between operations  14.9 us (5%)
  starting transfers between devices  8.58 us (3%)
    ppermute x3, waiting for transfers between devices, to_front(): return lax.ppermute(block, axis, [(i, i - 1) for i in range(1, n)])  60.5 us
    ppermute x3, waiting for transfers between devices, exchange(): return lax.ppermute(block, axis, [(i, partner(i, k, n)) for i in range(n)])  45 us
    all_gather x1, waiting for transfers between devices, body(): input_all = lax.all_gather(next_input, 'mp', axis=1, tiled=True)  42.9 us
    all_to_all x1, blocking collectives, body(): lax.all_to_all(new_weight, 'mp', split_axis=1, concat_axis=0, tiled=True)  31.3 us
    all_gather x1, waiting for transfers between devices, body(): weight_cols = lax.all_gather(weight_part, 'dp', axis=1, tiled=True)  25.5 us
    broadcast_in_dim x2, local copies, waits for them, and re-layouts, mine(): return lax.dynamic_slice_in_dim(rows, begin, shard_rows, 0)[None]  11.4 us
    dot_general x1, matrix products, body(): lax.dot_general(activations, out_grad, (((0,), (0,)), ((), ())), preferre...  10.7 us
    convert_element_type x3, other arithmetic, mine(): behind = to_front(block.astype(jnp.bfloat16), 'dp').astype(block.dtype)  8.57 us
  transfers between devices with their start and end apart: 8, of which 7 were waited for; matrix products, arithmetic and copies ran while one was open for 10% of the time, Pallas kernels for 0%

commit v1 on v0

--- a/solution.py
+++ b/solution.py
@@ -46,7 +46,15 @@
     new_second = 0.95 * old_second[0] + 0.05 * grad * grad
     update = new_first / first_fix / (jnp.sqrt(new_second / second_fix) + 1e-08)
     new_weight = (old_weight[0].astype(jnp.float32) - 0.01 * update).astype(jnp.bfloat16)
-    weight_part = lax.all_to_all(new_weight, "mp", split_axis=1, concat_axis=0, tiled=True)
+    weight_part = jnp.concatenate(
+        jax.lax.all_to_all(
+            jnp.stack(jnp.split(new_weight, jax.lax.axis_size("mp"), 1), 0),
+            axis_name="mp",
+            split_axis=0,
+            concat_axis=0,
+        ),
+        0,
+    )
     heads = lax.axis_size("mp")
     weight_part = weight_part.reshape(heads, old_rows, -1)
     weight_cols = lax.all_gather(weight_part, "dp", axis=1, tiled=True)

time: 293 us -> 245 us (0.84)
  waiting for transfers between devices: 175 us -> 132 us
  local copies, waits for them, and re-layouts: 27.4 us -> 20.9 us
    all_gather x1, waiting for transfers between devices: 42.9 us -> 0.01 us  [body(): input_all = lax.all_gather(next_input, 'mp', axis=1, tiled=True)]
    all_gather x1 -> x0, local copies, waits for them, and re-layouts: 6.49 us -> none  [body(): weight_cols = lax.all_gather(weight_part, 'dp', axis=1, tiled=True)]
    unnamed x21 -> x26, local copies, waits for them, and re-layouts: 5.95 us -> 5.72 us
  transfers between devices with their start and end apart: 8 -> 8, of which waited for: 7 -> 6; matrix products, arithmetic and copies ran while one was open for 10% -> 12% of each run, Pallas kernels for 0% -> 0%
where the time goes in v1:
time: 245 us
  waiting for transfers between devices  132 us (54%)
  blocking collectives  31.5 us (13%)
  local copies, waits for them, and re-layouts  20.9 us (9%)
  matrix products  20.2 us (8%)
  other arithmetic  17.1 us (7%)
  between operations  14.9 us (6%)
  starting transfers between devices  8.59 us (4%)
    ppermute x3, waiting for transfers between devices, to_front(): return lax.ppermute(block, axis, [(i, i - 1) for i in range(1, n)])  60.5 us
    ppermute x3, waiting for transfers between devices, exchange(): return lax.ppermute(block, axis, [(i, partner(i, k, n)) for i in range(n)])  44.5 us
    all_to_all x1, blocking collectives, body(): jax.lax.all_to_all(jnp.stack(jnp.split(new_weight, jax.lax.axis_size('mp'...  31.5 us
    all_gather x1, waiting for transfers between devices, body(): weight_cols = lax.all_gather(weight_part, 'dp', axis=1, tiled=True)  26.6 us
    dot_general x1, matrix products, body(): lax.dot_general(activations, out_grad, (((0,), (0,)), ((), ())), preferre...  12.1 us
    broadcast_in_dim x2, local copies, waits for them, and re-layouts, mine(): return lax.dynamic_slice_in_dim(rows, begin, shard_rows, 0)[None]  11.4 us
    convert_element_type x3, other arithmetic, mine(): behind = to_front(block.astype(jnp.bfloat16), 'dp').astype(block.dtype)  8.67 us
    dot_general x1, matrix products, body(): jnp.dot(input_all, weight_cols, preferred_element_type=jnp.float32)  8.05 us
  transfers between devices with their start and end apart: 8, of which 6 were waited for; matrix products, arithmetic and copies ran while one was open for 12% of the time, Pallas kernels for 0%

profile of v1, /device:TPU:0, one launch (start us, length us, event | category | flops | bytes accessed | tf_op | source)
XLA Modules:
  0.0 244.8 jit_solution(1601410080283354524)
XLA Ops:
  7.2 0.0 copy-start
  7.2 0.0 all-gather.5.cloned.1.call-start
  7.2 1.0 copy-done
  8.2 12.1 %convolution_convert_fusion = bf16[256,8192]{1,0:T(8,128)(2,1)} fusion(bf16[1024,256]{1,0:T(8,128)(2,1)S(1)} %copy-done, bf16[1024,8192]{1,0:T(8,128)(2,1)} %param.8), kind=kOutput, calls=%fused_computation | convolution fusion | flops 4297064448 | bytes 21495808 | tf_op jit(solution)/shard_map/dot_general | solution.py:34
  20.3 3.6 %dynamic-slice_bitcast_fusion.2 = (bf16[64,8192]{1,0:T(8,128)(2,1)}, bf16[64,8192]{1,0:T(8,128)(2,1)}, bf16[64,8192]{1,0:T(8,128)(2,1)}) fusion(bf16[4,64,8192]{2,1,0:T(8,128)(2,1)} %bitcast.68, s32[]{:T(128)S(6)} %select_n.19, s32[]{:T(128)S(6)} %select_n.21, s32[]{:T(128)S(6)} %select_n.20), kind=kLoop, calls=%fused_computation.25 | loop fusion | bytes 6291468 | tf_op jit(solution)/shard_map/jit(dynamic_index_in_dim)/squeeze | solution.py:40
  23.9 3.9 %collective-permute-start.2 = (bf16[64,8192]{1,0:T(8,128)(2,1)}, bf16[64,8192]{1,0:T(8,128)(2,1)S(1)}, u32[]{:S(2)}, u32[]{:S(2)}) collective-permute-start(bf16[64,8192]{1,0:T(8,128)(2,1)} %get-tuple-element.15), channel_id=1, source_target_pairs={{0,24},{8,16},{16,8},{24,0},{1,25},{9,17},{17,9},{25,1},{2,26},{10... | collective-permute-start | bytes 3145736 | tf_op jit(solution)/shard_map/ppermute | solution.py:13
  27.8 0.5 collective-permute-start.1
  28.3 0.1 collective-permute-start
  28.4 0.0 all-gather.5.cloned.1.call-update
  28.4 0.0 all-gather.3.cloned.1.call-start
  29.2 0.0 copy-start.8
  29.2 22.9 %collective-permute-done.2 = bf16[64,8192]{1,0:T(8,128)(2,1)S(1)} collective-permute-done((bf16[64,8192]{1,0:T(8,128)(2,1)}, bf16[64,8192]{1,0:T(8,128)(2,1)S(1)}, u32[]{:S(2)}, u32[]{:S(2)}) %collective-permute-start.2) | collective-permute-done | bytes 1048608 | tf_op jit(solution)/shard_map/ppermute | solution.py:13
  52.1 0.0 copy-start.6
  52.1 21.6 %collective-permute-done.1 = bf16[64,8192]{1,0:T(8,128)(2,1)S(1)} collective-permute-done((bf16[64,8192]{1,0:T(8,128)(2,1)}, bf16[64,8192]{1,0:T(8,128)(2,1)S(1)}, u32[]{:S(2)}, u32[]{:S(2)}) %collective-permute-start.1) | collective-permute-done | bytes 1048608 | tf_op jit(solution)/shard_map/ppermute | solution.py:13
  73.6 0.0 copy-done.6
  73.6 0.0 copy-start.7
  73.7 1.0 copy-done.7
  74.6 0.0 collective-permute-done
  74.6 5.9 %fusion.19 = (bf16[64,8192]{1,0:T(8,128)(2,1)}, f32[64,8192]{1,0:T(8,128)S(1)}, bf16[64,8192]{1,0:T(8,128)(2,1)}, f32[64,8192]{1,0:T(8,128)S(1)}) fusion(bf16[64,8192]{1,0:T(8,128)(2,1)} %copy-done.6, bf16[64,8192]{1,0:T(8,128)(2,1)} %copy-done.7, bf16[64,8192]{1,0:T(8,128)(2,1)} %collective-permute-done, bf16[4,64,8192]{2,1,0:T(8,128)(2,1)} %bitcast.69, ...), kind=kLoop, calls=%fused_computation.44 | loop fusion | flops 8388608 | bytes 14680068 | tf_op jit(solution)/shard_map/convert_element_type | solution.py:65
  80.6 0.0 copy-start.2
  80.6 0.0 copy-done.8
  80.6 1.1 fusion.7
  81.6 0.2 copy-done.2
  81.9 0.0 copy-start.5
  82.0 0.9 copy-done.5
  82.9 31.5 %all_to_all.5 = bf16[8,64,1024]{2,1,0:T(8,128)(2,1)} all-to-all(bf16[8,64,1024]{2,1,0:T(8,128)(2,1)S(1)} %fusion.11), channel_id=1, replica_groups=mesh['dp'=4,'mp'=8] {'mp'}, dimensions={0} | all-to-all | bytes 2097152 | tf_op jit(solution)/shard_map/all_to_all | solution.py:50
  114.4 0.0 all-gather.3.cloned.1.call-update
  114.4 1.3 collective-permute-start.5
  115.7 1.3 collective-permute-start.4
  117.0 0.1 pad_dynamic-slice_fusion.7
  117.1 0.1 pad_dynamic-slice_fusion.6
  117.2 1.5 collective-permute-start.3
  118.7 35.3 %collective-permute-done.5 = bf16[64,8192]{1,0:T(8,128)(2,1)} collective-permute-done((bf16[64,8192]{1,0:T(8,128)(2,1)}, bf16[64,8192]{1,0:T(8,128)(2,1)}, u32[]{:S(2)}, u32[]{:S(2)}) %collective-permute-start.5) | collective-permute-done | bytes 1048608 | tf_op jit(solution)/shard_map/ppermute | solution.py:23
  153.9 1.4 convert_element_type.62
  155.3 0.0 copy-start.3
  155.3 21.1 %collective-permute-done.4 = bf16[64,8192]{1,0:T(8,128)(2,1)} collective-permute-done((bf16[64,8192]{1,0:T(8,128)(2,1)}, bf16[64,8192]{1,0:T(8,128)(2,1)}, u32[]{:S(2)}, u32[]{:S(2)}) %collective-permute-start.4) | collective-permute-done | bytes 1048608 | tf_op jit(solution)/shard_map/ppermute | solution.py:23
  176.4 1.4 convert_element_type.60
  177.8 0.0 copy-done.3
  177.8 4.0 %fusion.1 = (f32[86,8192]{1,0:T(8,128)}, f32[86,8192]{1,0:T(8,128)}) fusion(s32[]{:T(128)S(6)} %select_n.22, f32[64,8192]{1,0:T(8,128)S(1)} %get-tuple-element.9, f32[64,8192]{1,0:T(8,128)S(1)} %convert_element_type.62, f32[86]{0:T(128)S(1)} %pad_dynamic-slice_fusion.6, f32[64,8192]{1,0:T(8,128)S(1)} %convert_element_type.60, f32[64,8192]{1,0:T(8,128)S(1)} %copy-done.3), kind=kLoop, calls=%fused_computation.9 | loop fusion | flops 2818048 | bytes 14025052 | tf_op jit(solution)/shard_map/concatenate | solution.py:66
  181.8 6.7 %broadcast_in_dim.14 = f32[1,86,8192]{2,0,1:T(1,128)} reshape(f32[86,8192]{1,0:T(8,128)} %get-tuple-element.18) | data formatting | bytes 5636096 | tf_op jit(solution)/shard_map/broadcast_in_dim | solution.py:67
  188.5 0.0 copy-done.4
  188.5 4.7 %broadcast_in_dim.15 = f32[1,86,8192]{2,0,1:T(1,128)} reshape(f32[86,8192]{1,0:T(8,128)S(1)} %copy-done.4) | data formatting | bytes 5636096 | tf_op jit(solution)/shard_map/broadcast_in_dim | solution.py:67
  193.2 4.1 %collective-permute-done.3 = bf16[64,8192]{1,0:T(8,128)(2,1)} collective-permute-done((bf16[64,8192]{1,0:T(8,128)(2,1)}, bf16[64,8192]{1,0:T(8,128)(2,1)}, u32[]{:S(2)}, u32[]{:S(2)}) %collective-permute-start.3) | collective-permute-done | bytes 1048608 | tf_op jit(solution)/shard_map/ppermute | solution.py:23
  197.3 3.4 %fusion.10 = bf16[1,86,8192]{2,1,0:T(8,128)(2,1)} fusion(s32[]{:T(128)S(6)} %select_n.22, bf16[64,8192]{1,0:T(8,128)(2,1)} %copy-done.5, bf16[64,8192]{1,0:T(8,128)(2,1)} %collective-permute-done.3, bf16[86]{0:T(256)(128)(2,1)S(1)} %pad_dynamic-slice_fusion.7), kind=kLoop, calls=%fused_computation.22 | loop fusion | flops 4227072 | bytes 3506352 | tf_op jit(solution)/shard_map/broadcast_in_dim | solution.py:67
  200.7 26.6 %all-gather.3.cloned.1.call-done = bf16[8,256,1024]{2,1,0:T(8,128)(2,1)} async-done(((bf16[8,64,1024]{2,1,0:T(8,128)(2,1)}), bf16[8,256,1024]{2,1,0:T(8,128)(2,1)}) %all-gather.3.cloned.1.call-update) | async-done | bytes 4194320 | tf_op jit(solution)/shard_map/all_gather | solution.py:60
  227.3 8.0 %convert_bitcast_fusion = bf16[1024,1024]{0,1:T(8,128)(2,1)S(1)} fusion(bf16[2048,1024]{1,0:T(8,128)(2,1)} %bitcast.70, bf16[1024,2048]{1,0:T(8,128)(2,1)} %all-gather.5.cloned.1.call-done), kind=kOutput, calls=%fused_computation.19 | convolution fusion | flops 4296015872 | bytes 10485760 | tf_op jit(solution)/shard_map/dot_general | solution.py:70
  235.4 2.6 %copy.11 = bf16[1024,1024]{1,0:T(8,128)(2,1)} copy(bf16[1024,1024]{0,1:T(8,128)(2,1)S(1)} %convert_bitcast_fusion) | data formatting | bytes 4194304
  237.9 0.0 copy-done.1
  (13 shorter events, 0.1 us)
Async XLA Ops:
  7.2 1.1 copy-start
  7.2 193.5 %all-gather.5.cloned.1.call-start = ((), (), s32[]{:S(2)}) async-start(), calls=%async_computation.2 | async-start | bytes 4718592 | tf_op jit(solution)/shard_map/all_gather | solution.py:33
  23.9 28.1 %collective-permute-start.2 = (bf16[64,8192]{1,0:T(8,128)(2,1)}, bf16[64,8192]{1,0:T(8,128)(2,1)S(1)}, u32[]{:S(2)}, u32[]{:S(2)}) collective-permute-start(bf16[64,8192]{1,0:T(8,128)(2,1)} %get-tuple-element.15), channel_id=1, source_target_pairs={{0,24},{8,16},{16,8},{24,0},{1,25},{9,17},{17,9},{25,1},{2,26},{10... | collective-permute-start | bytes 3145736 | tf_op jit(solution)/shard_map/ppermute | solution.py:13
  27.8 45.8 %collective-permute-start.1 = (bf16[64,8192]{1,0:T(8,128)(2,1)}, bf16[64,8192]{1,0:T(8,128)(2,1)S(1)}, u32[]{:S(2)}, u32[]{:S(2)}) collective-permute-start(bf16[64,8192]{1,0:T(8,128)(2,1)} %get-tuple-element.16), channel_id=1, source_target_pairs={{0,16},{8,24},{16,0},{24,8},{1,17},{9,25},{17,1},{25,9},{2,18},{10... | collective-permute-start | bytes 3145736 | tf_op jit(solution)/shard_map/ppermute | solution.py:13
  28.3 46.3 %collective-permute-start = (bf16[64,8192]{1,0:T(8,128)(2,1)}, bf16[64,8192]{1,0:T(8,128)(2,1)}, u32[]{:S(2)}, u32[]{:S(2)}) collective-permute-start(bf16[64,8192]{1,0:T(8,128)(2,1)} %get-tuple-element.14), channel_id=1, source_target_pairs={{0,8},{8,0},{16,24},{24,16},{1,9},{9,1},{17,25},{25,17},{2,10},{10... | collective-permute-start | bytes 3145736 | tf_op jit(solution)/shard_map/ppermute | solution.py:13
  28.4 198.9 %all-gather.3.cloned.1.call-start = ((), (), s32[]{:S(2)}) async-start(), calls=%async_computation.1 | async-start | bytes 5242880 | tf_op jit(solution)/shard_map/all_gather | solution.py:60
  29.2 51.4 %copy-start.8 = (bf16[1,64,8192]{2,1,0:T(8,128)(2,1)S(1)}, bf16[1,64,8192]{2,1,0:T(8,128)(2,1)}, u32[]{:S(2)}) copy-start(bf16[1,64,8192]{2,1,0:T(8,128)(2,1)} %param.9) | copy-start | bytes 3145732
  52.1 21.6 %copy-start.6 = (bf16[64,8192]{1,0:T(8,128)(2,1)}, bf16[64,8192]{1,0:T(8,128)(2,1)S(1)}, u32[]{:S(2)}) copy-start(bf16[64,8192]{1,0:T(8,128)(2,1)S(1)} %collective-permute-done.2) | copy-start | bytes 3145732
  73.6 1.0 copy-start.7
  80.6 1.3 copy-start.2
  81.9 1.0 copy-start.5
  114.4 39.5 %collective-permute-start.5 = (bf16[64,8192]{1,0:T(8,128)(2,1)}, bf16[64,8192]{1,0:T(8,128)(2,1)}, u32[]{:S(2)}, u32[]{:S(2)}) collective-permute-start(bf16[64,8192]{1,0:T(8,128)(2,1)} %get-tuple-element.8), channel_id=1, source_target_pairs={{8,0},{16,8},{24,16},{9,1},{17,9},{25,17},{10,2},{18,10},{26,18},{... | collective-permute-start | bytes 3145736 | tf_op jit(solution)/shard_map/ppermute | solution.py:23
  115.7 60.7 %collective-permute-start.4 = (bf16[64,8192]{1,0:T(8,128)(2,1)}, bf16[64,8192]{1,0:T(8,128)(2,1)}, u32[]{:S(2)}, u32[]{:S(2)}) collective-permute-start(bf16[64,8192]{1,0:T(8,128)(2,1)} %get-tuple-element.12), channel_id=1, source_target_pairs={{8,0},{16,8},{24,16},{9,1},{17,9},{25,17},{10,2},{18,10},{26,18},{... | collective-permute-start | bytes 3145736 | tf_op jit(solution)/shard_map/ppermute | solution.py:23
  117.2 80.1 %collective-permute-start.3 = (bf16[64,8192]{1,0:T(8,128)(2,1)}, bf16[64,8192]{1,0:T(8,128)(2,1)}, u32[]{:S(2)}, u32[]{:S(2)}) collective-permute-start(bf16[64,8192]{1,0:T(8,128)(2,1)} %copy-done.5), channel_id=1, source_target_pairs={{8,0},{16,8},{24,16},{9,1},{17,9},{25,17},{10,2},{18,10},{26,18},{... | collective-permute-start | bytes 3145736 | tf_op jit(solution)/shard_map/ppermute | solution.py:23
  155.3 22.5 %copy-start.3 = (f32[64,8192]{1,0:T(8,128)S(1)}, f32[64,8192]{1,0:T(8,128)}, u32[]{:S(2)}) copy-start(f32[64,8192]{1,0:T(8,128)} %copy-done.2) | copy-start | bytes 6291460
  181.8 6.7 %copy-start.4 = (f32[86,8192]{1,0:T(8,128)S(1)}, f32[86,8192]{1,0:T(8,128)}, u32[]{:S(2)}) copy-start(f32[86,8192]{1,0:T(8,128)} %get-tuple-element.17) | copy-start | bytes 8454148
  227.3 10.6 %copy-start.1 = (bf16[1024,256]{1,0:T(8,128)(2,1)S(1)}, bf16[1024,256]{1,0:T(8,128)(2,1)}, u32[]{:S(2)}) copy-start(bf16[1024,256]{1,0:T(8,128)(2,1)} %param.7) | copy-start | bytes 1572868
Sparse Core Ops, SparseCore 0:
  28.5 49.5 all-gather.4
  114.5 112.7 all-gather.2
